TPU v7x, 32 devices: a whole 2x2x4 slice. The times are simulated.
32 devices in a mesh: row: 4 (over z), col: 8 (over y, x, core).
Axes of the slice: x: 2, y: 2, z: 4, core: 2. Of those that a mesh axis runs over, the one named last changes fastest.
Arguments:
- images: bfloat16 [8, 32, 65536], P(None, 'row', 'col'), may hold values from -6 to 6
- kernel: bfloat16 [3, 3, 1024, 1024], P(None, None, 'col', 'row'), may hold values from -0.09375 to 0.09375
- upstream: bfloat16 [8, 32, 65536], P(None, 'row', 'col'), may hold values from -6 to 6
Outputs:
- output_maps: bfloat16 [8, 32, 65536], P(None, 'row', 'col')
- input_grad: bfloat16 [8, 32, 65536], P(None, 'row', 'col')
- kernel_grad: float32 [3, 3, 1024, 1024], P(None, None, 'col', 'row')
All inputs are finite; a program needn't handle non-finite values.
Results may differ from a plain program's by a relative error of at most 0.001.
Values may be sent and summed in bfloat16 or wider, within the bound.
A program may use at most 128 MiB of HBM per device.

v0:
```python
import functools

import jax
import jax.numpy as jnp
from jax import lax
from jax.experimental import pallas as pl
from jax.experimental.pallas import tpu as pltpu
from jax.sharding import PartitionSpec as P

W = 64
MESH = pl.DeviceIdType.MESH
F32 = jnp.float32
BF16 = jnp.bfloat16


def remote(src, dst, send, recv, row, col):
    return pltpu.make_async_remote_copy(
        src_ref=src, dst_ref=dst, send_sem=send, recv_sem=recv, device_id=(row, col), device_id_type=MESH
    )


def shift_sum(low, mid, high, width):
    rows = low.shape[0]
    at = lax.rem(lax.broadcasted_iota(jnp.int32, low.shape, 0), jnp.int32(width))
    first = jnp.where(at == 0, 0.0, pltpu.roll(low, 1, 0))
    last = jnp.where(at == width - 1, 0.0, pltpu.roll(high, rows - 1, 0))
    return first + mid + last


def kernel(
    n_row, x_ref, g_ref, w_ref, out_ref, ig_ref, kg_ref,
    xg, gg, wf, wb, halo, turned, kgp, kgr, kgz, stage,
    own_sem, ax_send, ax_recv, hz_send, hz_recv, hc_send, hc_recv,
    wz_send, wz_recv, wp_send, wp_recv, wc_send, wc_recv, wq_send, wq_recv,
    kp_send, kp_recv, kz_send, kz_recv, op_send, op_recv,
):
    batch, height, width, ch = x_ref.shape
    half = batch // 2
    pair = 2 * ch
    taps = w_ref.shape[0]
    row, col = lax.axis_index("row"), lax.axis_index("col")
    chip, core = col // 2, lax.rem(col, 2)
    mate = chip * 2 + 1 - core

    def chip_at(t):
        cx, cy = lax.rem(chip, 2), chip // 2
        return lax.rem(cy + t // 2, 2) * 2 + lax.rem(cx + t % 2, 2)

    chips = [chip_at(t) for t in range(4)]
    peers = [(t, k) for t in range(4) for k in range(2) if (t, k) != (0, 0)]

    def peer(t, k):
        return chips[t] * 2 + lax.rem(core + k, 2)

    def row_at(s):
        return lax.rem(row + s, n_row)

    barrier = pltpu.get_barrier_semaphore()
    for t, k in peers:
        pl.semaphore_signal(barrier, inc=1, device_id=(row, peer(t, k)), device_id_type=MESH)
    for s in range(1, n_row):
        pl.semaphore_signal(barrier, inc=1, device_id=(row_at(s), col), device_id_type=MESH)
    pl.semaphore_wait(barrier, len(peers) + n_row - 1)

    def lanes(c, size):
        return pl.ds(pl.multiple_of(c * size, size), size)

    own = pl.ds(core * half, half)
    arrays = ((x_ref, xg), (g_ref, gg))
    has_up, has_down = row > 0, row < n_row - 1

    def body_copy(n, t, k, source):
        src, dst = arrays[n]
        to = peer(t, k)
        return remote(
            src.at[pl.ds(lax.rem(core + k, 2) * half, half)],
            dst.at[:, pl.ds(1, height), :, lanes(source, ch)],
            ax_send.at[n, t, k], ax_recv.at[n, t, k], row, to,
        )

    def halo_z(n, side):
        src, _ = arrays[n]
        at = height - 1 if side == 0 else 0
        to = row + 1 if side == 0 else row - 1
        return remote(src.at[:, pl.ds(at, 1)], halo.at[n, side], hz_send.at[n, side], hz_recv.at[n, side], to, col)

    def halo_c(n, side, t, k, source):
        _, dst = arrays[n]
        at = 0 if side == 0 else height + 1
        return remote(
            halo.at[n, side, pl.ds(lax.rem(core + k, 2) * half, half)],
            dst.at[:, pl.ds(at, 1), :, lanes(source, ch)],
            hc_send.at[n, side, t, k], hc_recv.at[n, side, t, k], row, peer(t, k),
        )

    def halo_own(n, side):
        _, dst = arrays[n]
        at = 0 if side == 0 else height + 1
        return pltpu.make_async_copy(
            halo.at[n, side, own], dst.at[:, pl.ds(at, 1), :, lanes(col, ch)], hc_send.at[n, side, 0, 0]
        )

    def weights_z(s, source):
        return remote(
            w_ref, wf.at[:, lanes(core, ch), lanes(source, pair)], wz_send.at[s], wz_recv.at[s], row_at(s), col
        )

    def has(side):
        return has_up if side == 0 else has_down

    @pl.when(has_down)
    def _():
        for n in range(2):
            halo_z(n, 0).start()

    @pl.when(has_up)
    def _():
        for n in range(2):
            halo_z(n, 1).start()

    own_copies = [
        pltpu.make_async_copy(x_ref.at[own], xg.at[:, pl.ds(1, height), :, lanes(col, ch)], own_sem.at[0]),
        pltpu.make_async_copy(g_ref.at[own], gg.at[:, pl.ds(1, height), :, lanes(col, ch)], own_sem.at[1]),
        pltpu.make_async_copy(w_ref, wf.at[:, lanes(core, ch), lanes(row, pair)], own_sem.at[2]),
    ]
    for copy in own_copies:
        copy.start()
    body_copy(1, 0, 1, col).start()
    for t, k in peers:
        body_copy(0, t, k, col).start()
    for s in range(1, n_row):
        weights_z(s, row).start()

    @pl.when(jnp.logical_not(has_up))
    def _():
        xg[:, 0] = jnp.zeros((half, width, xg.shape[3]), BF16)
        gg[:, 0] = jnp.zeros((half, width, xg.shape[3]), BF16)

    @pl.when(jnp.logical_not(has_down))
    def _():
        xg[:, height + 1] = jnp.zeros((half, width, xg.shape[3]), BF16)
        gg[:, height + 1] = jnp.zeros((half, width, xg.shape[3]), BF16)

    def spread_halo(n):
        for side in range(2):
            @pl.when(has(side))
            def _():
                halo_z(n, side).wait_recv()
                halo_own(n, side).start()
                for t, k in peers:
                    halo_c(n, side, t, k, col).start()

    spread_halo(0)
    for t, k in peers:
        if t:
            body_copy(1, t, k, col).start()
    spread_halo(1)

    own_copies[0].wait()
    own_copies[1].wait()
    body_copy(1, 0, 1, mate).wait_recv()

    def turn(b, _):
        block = gg[b, pl.ds(1, height), :, lanes(chip, pair)].astype(F32).reshape(height * width, pair)
        at = lax.rem(lax.broadcasted_iota(jnp.int32, block.shape, 0), jnp.int32(width))
        rows = height * width
        left = jnp.where(at == width - 1, 0.0, pltpu.roll(block, rows - 1, 0))
        right = jnp.where(at == 0, 0.0, pltpu.roll(block, 1, 0))
        where = pl.ds(pl.multiple_of(b * rows, rows), rows)
        for c, part in enumerate((left, block, right)):
            turned[c * pair:(c + 1) * pair, where] = part.T.astype(BF16)
        return 0

    lax.fori_loop(0, half, turn, 0)

    def wait_halos(n, t):
        for side in range(2):
            @pl.when(has(side))
            def _():
                for k in range(2):
                    if (t, k) == (0, 0):
                        halo_own(n, side).wait()
                    else:
                        halo_c(n, side, t, k, peer(t, k)).wait_recv()

    def mate_part(t):
        theirs = pl.ds(pl.multiple_of((1 - core) * ch, ch), ch)
        return remote(kgp.at[t, :, theirs], kgr.at[t], kp_send.at[t], kp_recv.at[t], row, mate)

    def z_part(t, to, slot):
        mine = pl.ds(pl.multiple_of(core * ch, ch), ch)
        return remote(kgp.at[t, :, mine], kgz.at[slot], kz_send.at[t], kz_recv.at[slot], to, col)

    def hand_on(t):
        mate_part(t).wait_recv()
        mine = pl.ds(pl.multiple_of(core * ch, ch), ch)

        def add(i, _):
            kgp[t, i, mine] = kgp[t, i, mine] + kgr[t, i]
            return 0

        lax.fori_loop(0, taps, add, 0)

        @pl.when(chips[t] != row)
        def _():
            z_part(t, chips[t], row).start()

        @pl.when(chips[t] == row)
        def _():
            def keep(i, _):
                kg_ref[i] = kgp[t, i, mine]
                return 0

            lax.fori_loop(0, taps, keep, 0)

    for t in range(4):
        for k in range(2):
            if (t, k) != (0, 0):
                body_copy(0, t, k, peer(t, k)).wait_recv()
        wait_halos(0, t)

        def tap_row(a, _):
            window = xg[:, pl.ds(a, height), :, lanes(chips[t], pair)].reshape(half * height * width, pair)
            part = jnp.dot(turned[...], window, preferred_element_type=F32)
            for c in range(3):
                kgp[t, a * 3 + c] = part[c * pair:(c + 1) * pair]
            return 0

        lax.fori_loop(0, 3, tap_row, 0)
        mate_part(t).start()
        if t:
            hand_on(t - 1)
    hand_on(3)

    own_copies[2].wait()
    for s in range(1, n_row):
        weights_z(s, lax.rem(row + n_row - s, n_row)).wait_recv()

    def weights_mate(k):
        mine = lanes(core if k == 0 else 1 - core, ch)
        return remote(wf.at[:, mine], wf.at[:, mine], wp_send, wp_recv, row, mate)

    def weights_c(t, source):
        return remote(
            wf.at[:, lanes(core, ch), lanes(chips[t], pair)], wb.at[:, lanes(source, ch)],
            wc_send.at[t], wc_recv.at[t], row, peer(t, 0),
        )

    weights_mate(0).start()
    wb_own = pltpu.make_async_copy(wf.at[:, lanes(core, ch), lanes(chip, pair)], wb.at[:, lanes(col, ch)], own_sem.at[3])
    wb_own.start()
    for t in range(1, 4):
        weights_c(t, col).start()

    def weights_pass(t, k):
        rows = lanes(peer(t, k), ch)
        return remote(wb.at[:, rows], wb.at[:, rows], wq_send.at[t], wq_recv.at[t], row, mate)

    def convolve(grid_ref, weights, dims, flip, result, n):
        def image(b, _):
            sums = []
            for c in range(3):
                total = None
                for a in range(3):
                    block = grid_ref[b, pl.ds(2 - a if flip else a, height)].reshape(height * width, grid_ref.shape[3])
                    part = lax.dot_general(block, weights[a * 3 + c], (dims, ((), ())), preferred_element_type=F32)
                    total = part if total is None else total + part
                sums.append(total)
            if flip:
                sums = sums[::-1]
            value = shift_sum(*sums, width).astype(BF16).reshape(height, width, pair)

            @pl.when(core == 0)
            def _():
                result[b] = value[:, :, :ch]
                stage[n, b] = value[:, :, ch:]

            @pl.when(core == 1)
            def _():
                result[half + b] = value[:, :, ch:]
                stage[n, b] = value[:, :, :ch]

            return 0

        lax.fori_loop(0, half, image, 0)

    def result_mate(n, result, batch_half):
        return remote(
            stage.at[n], result.at[pl.ds(batch_half * half, half)], op_send.at[n], op_recv.at[n], row, mate
        )

    weights_mate(1).wait_recv()
    convolve(xg, wf, ((1,), (1,)), False, out_ref, 0)
    result_mate(0, out_ref, core).start()

    wb_own.wait()
    weights_pass(0, 0).start()
    for t in range(1, 4):
        weights_c(t, peer(t, 0)).wait_recv()
        weights_pass(t, 0).start()
    for t in range(1, 4):
        for k in range(2):
            body_copy(1, t, k, peer(t, k)).wait_recv()
    for t in range(4):
        wait_halos(1, t)
    for t in range(4):
        weights_pass(t, 1).wait_recv()
    convolve(gg, wb, ((1,), (0,)), True, ig_ref, 1)
    result_mate(1, ig_ref, core).start()

    for s in range(1, n_row):
        z_part(0, row, row_at(s)).wait_recv()

        def add(i, _):
            kg_ref[i] = kg_ref[i] + kgz[row_at(s), i]
            return 0

        lax.fori_loop(0, taps, add, 0)

    for n in range(2):
        for t, k in peers:
            body_copy(n, t, k, col).wait_send()
        for side in range(2):
            @pl.when(has(1 - side))
            def _():
                halo_z(n, side).wait_send()

            @pl.when(has(side))
            def _():
                for t, k in peers:
                    halo_c(n, side, t, k, col).wait_send()
    for s in range(1, n_row):
        weights_z(s, row).wait_send()
    weights_mate(0).wait_send()
    for t in range(1, 4):
        weights_c(t, col).wait_send()
    for t in range(4):
        weights_pass(t, 0).wait_send()
        mate_part(t).wait_send()

        @pl.when(chips[t] != row)
        def _():
            z_part(t, chips[t], row).wait_send()

    result_mate(0, out_ref, core).wait_send()
    result_mate(1, ig_ref, core).wait_send()
    result_mate(0, out_ref, 1 - core).wait_recv()
    result_mate(1, ig_ref, 1 - core).wait_recv()


def fused(images, upstream, weights):
    n_row, n_col = lax.axis_size("row"), lax.axis_size("col")
    batch, height, width, ch = images.shape
    taps, pair, half = weights.shape[0], 2 * ch, batch // 2
    every = ch * n_col
    dma = pltpu.SemaphoreType.DMA
    vmem = pl.BlockSpec(memory_space=pltpu.VMEM)
    grid = (half, height + 2, width, every)
    flops = 3 * 2 * half * height * width * every * pair * taps
    return pl.pallas_call(
        functools.partial(kernel, n_row),
        out_shape=(
            jax.ShapeDtypeStruct(images.shape, BF16),
            jax.ShapeDtypeStruct(images.shape, BF16),
            jax.ShapeDtypeStruct(weights.shape, F32),
        ),
        in_specs=[vmem] * 3,
        out_specs=(vmem,) * 3,
        scratch_shapes=[
            pltpu.VMEM(grid, BF16),
            pltpu.VMEM(grid, BF16),
            pltpu.VMEM((taps, pair, every), BF16),
            pltpu.VMEM((taps, every, pair), BF16),
            pltpu.VMEM((2, 2, batch, 1, width, ch), BF16),
            pltpu.VMEM((3 * pair, half * height * width), BF16),
            pltpu.VMEM((4, taps, pair, pair), F32),
            pltpu.VMEM((4, taps, ch, pair), F32),
            pltpu.VMEM((n_row, taps, ch, pair), F32),
            pltpu.VMEM((2, half, height, width, ch), BF16),
            dma((4,)),
            dma((2, 4, 2)), dma((2, 4, 2)),
            dma((2, 2)), dma((2, 2)),
            dma((2, 2, 4, 2)), dma((2, 2, 4, 2)),
            dma((n_row,)), dma((n_row,)),
            dma, dma,
            dma((4,)), dma((4,)),
            dma((4,)), dma((4,)),
            dma((4,)), dma((4,)),
            dma((4,)), dma((n_row,)),
            dma((2,)), dma((2,)),
        ],
        compiler_params=pltpu.CompilerParams(
            collective_id=0, has_side_effects=True, vmem_limit_bytes=60 * 1024 * 1024
        ),
        cost_estimate=pl.CostEstimate(flops=flops, bytes_accessed=8 * 1024 * 1024, transcendentals=0),
    )(images, upstream, weights)


def fits(n_row, n_col, images, kernel_block):
    ch = images.shape[2] // W
    return (
        n_row == 4 and n_col == 8 and ch == 128 and images.shape[0] % 2 == 0
        and kernel_block.shape[2] == ch and kernel_block.shape[3] == 2 * ch and images.size <= 8 * 8 * 8192
    )


def to_last(flat):
    return to_maps(flat).transpose(0, 1, 3, 2)


def from_last(maps):
    return to_flat(maps.transpose(0, 1, 3, 2))


def padded_2(block, sides, width):
    for axis, dim in sides:
        count = lax.axis_size(axis)
        forward = [(i, i + 1) for i in range(count - 1)]
        backward = [(target, source) for source, target in forward]
        low = lax.ppermute(
            lax.slice_in_dim(block, block.shape[dim] - width, None, axis=dim), axis, forward
        )
        high = lax.ppermute(lax.slice_in_dim(block, 0, width, axis=dim), axis, backward)
        block = jnp.concatenate([low, block, high], axis=dim)
    return block


def convolve_valid(inputs, weights, weight_spec):
    return lax.conv_general_dilated(
        inputs,
        weights,
        (1, 1),
        ((0, 0), (1, 1)),
        dimension_numbers=("NHCW", weight_spec, "NHCW"),
        preferred_element_type=jnp.float32,
    )


def to_maps(flat):
    return flat.reshape(flat.shape[0], flat.shape[1], flat.shape[2] // W, W)


def to_flat(maps):
    return maps.reshape(maps.shape[0], maps.shape[1], maps.shape[2] * maps.shape[3])


def gathered(images, kernel, upstream):
    weights_all = lax.all_gather(kernel, "row", axis=3, tiled=True)
    images_rim = padded_2(images, (("row", 1),), 1)
    grads_rim = padded_2(upstream, (("row", 1),), 1)
    grads_maps = to_maps(grads_rim)
    batch = images.shape[0]
    height = images.shape[1]
    width = W
    out_local = kernel.shape[2]
    grads_mid = grads_maps[:, 1:-1]
    output_init = jnp.zeros((batch, height, out_local, width), jnp.float32)
    output_sum = output_init
    panel_in = to_maps(lax.all_gather(images_rim, "col", axis=2, tiled=True))
    count_here = panel_in.shape[2]
    output_sum = output_sum + convolve_valid(panel_in, weights_all, "HWOI")
    padded = jnp.pad(panel_in, ((0, 0), (0, 0), (0, 0), (1, 1)))
    blocks = []
    for tap_row in range(3):
        for tap_col in range(3):
            window = padded[:, tap_row : tap_row + height, :, tap_col : tap_col + width]
            blocks.append(
                jnp.einsum("bhiw,bhow->oi", window, grads_mid, preferred_element_type=jnp.float32)
            )
    stacked = jnp.stack(blocks).reshape(3, 3, out_local, count_here)
    output_sum, weight_part = (output_sum, stacked)
    kernel_grad = lax.psum_scatter(weight_part, "row", scatter_dimension=3, tiled=True)
    flipped = jnp.flip(weights_all, (0, 1))
    partial_grad = to_flat(convolve_valid(grads_maps, flipped, "HWIO"))
    input_grad = lax.psum_scatter(partial_grad, "col", scatter_dimension=2, tiled=True)
    return (to_flat(output_sum).astype(jnp.bfloat16), input_grad.astype(jnp.bfloat16), kernel_grad)


def shards(images, kernel_block, upstream):
    if not fits(lax.axis_size("row"), lax.axis_size("col"), images, kernel_block):
        return gathered(images, kernel_block, upstream)
    taps = kernel_block.reshape((9,) + kernel_block.shape[2:])
    out, grad, kernel_grad = fused(to_last(images), to_last(upstream), taps)
    return from_last(out), from_last(grad), kernel_grad.reshape(kernel_block.shape)


def solution(mesh):
    return jax.shard_map(
        shards,
        mesh=mesh,
        in_specs=(P(None, "row", "col"), P(None, None, "col", "row"), P(None, "row", "col")),
        out_specs=(P(None, "row", "col"), P(None, "row", "col"), P(None, None, "col", "row")),
        check_vma=False,
    )
```

profile of v0, /device:TPU:8, one launch (start us, length us, event | category | flops | bytes accessed | tf_op | source)
XLA Modules:
  0.0 193.7 jit_solution(8397942903127118977)
XLA Ops:
  0.6 3.3 %reshape.24 = bf16[8,8,128,64]{3,2,1,0:T(8,128)(2,1)S(1)} reshape(bf16[8,8,8192]{2,1,0:T(8,128)(2,1)} %param.3) | data formatting | bytes 2097152 | tf_op jit(solution)/shard_map/reshape | solution.py:440
  3.9 0.0 copy-start.1
  3.9 1.6 copy.6
  5.5 0.0 copy-done.1
  5.5 2.3 %reshape.25 = bf16[8,8,128,64]{3,2,1,0:T(8,128)(2,1)S(1)} reshape(bf16[8,8,8192]{2,1,0:T(8,128)(2,1)S(1)} %copy-done.1) | data formatting | bytes 2097152 | tf_op jit(solution)/shard_map/reshape | solution.py:440
  7.8 1.6 copy.7
  9.4 175.1 %shard_map.58 = (bf16[8,8,64,128]{3,2,1,0:T(8,128)(2,1)}, bf16[8,8,64,128]{3,2,1,0:T(8,128)(2,1)}, f32[9,128,256]{2,1,0:T(8,128)}) custom-call(bf16[8,8,64,128]{3,2,1,0:T(8,128)(2,1)} %bitcast.12, bf16[8,8,64,128]{3,2,1,0:T(8,128)(2,1)} %bitcast.13, bf16[9,128,256]{2,1,0:T(8,128)(2,1)} %bitcast.15), custom_call_target="tpu_custom_call" | custom-call | flops 28991029248 | bytes 8388608 | tf_op jit(solution)/shard_map/pallas_call | solution.py:360
  184.6 2.0 %copy.9 = bf16[8,8,128,64]{3,2,1,0:T(8,128)(2,1)S(1)} copy(bf16[8,8,128,64]{2,3,1,0:T(8,128)(2,1)} %bitcast.14) | data formatting | bytes 2097152 | tf_op jit(solution)/shard_map/transpose | solution.py:412
  186.6 0.0 copy-start.2
  186.6 2.5 %reshape.28 = bf16[8,8,8192]{2,1,0:T(8,128)(2,1)} reshape(bf16[8,8,128,64]{3,2,1,0:T(8,128)(2,1)S(1)} %copy.9) | data formatting | bytes 2097152 | tf_op jit(solution)/shard_map/reshape | solution.py:444
  189.1 0.0 copy-done.2
  189.1 1.1 copy.8
  190.2 0.0 copy-start
  190.2 2.5 %reshape.27 = bf16[8,8,8192]{2,1,0:T(8,128)(2,1)} reshape(bf16[8,8,128,64]{3,2,1,0:T(8,128)(2,1)S(1)} %copy.8) | data formatting | bytes 2097152 | tf_op jit(solution)/shard_map/reshape | solution.py:444
  192.7 0.0 copy-done
  192.7 1.0 copy.11
Async XLA Ops:
  3.9 1.6 copy-start.1
  186.6 2.5 %copy-start.2 = (bf16[8,8,64,128]{3,2,1,0:T(8,128)(2,1)S(1)}, bf16[8,8,64,128]{3,2,1,0:T(8,128)(2,1)}, u32[]{:S(2)}) copy-start(bf16[8,8,64,128]{3,2,1,0:T(8,128)(2,1)} %get-tuple-element.6) | copy-start | bytes 3145732
  190.2 2.5 %copy-start = (f32[9,128,256]{2,1,0:T(8,128)S(1)}, f32[9,128,256]{2,1,0:T(8,128)}, u32[]{:S(2)}) copy-start(f32[9,128,256]{2,1,0:T(8,128)} %get-tuple-element.8) | copy-start | bytes 3538948
where the time goes:
time: 196 us; the launch traced here: 194 us
  Pallas kernels  175 us (89%)
  local copies, waits for them, and re-layouts  17.9 us (9%)
    pallas_call x1, Pallas kernels, fused(): pl.pallas_call(functools.partial(kernel, n_row), out_shape=(jax.ShapeDtyp...  175 us
    reshape x4, local copies, waits for them, and re-layouts, to_maps(): return flat.reshape(flat.shape[0], flat.shape[1], flat.shape[2] // W, W)  8.76 us
    reshape x2, local copies, waits for them, and re-layouts, to_flat(): maps.reshape(maps.shape[0], maps.shape[1], maps.shape[2] * maps.shape[3])  4.97 us

commit v1 on v0

--- a/solution.py
+++ b/solution.py
@@ -30,7 +30,7 @@
 def kernel(
     n_row, x_ref, g_ref, w_ref, out_ref, ig_ref, kg_ref,
     xg, gg, wf, wb, halo, turned, kgp, kgr, kgz, stage,
-    own_sem, ax_send, ax_recv, hz_send, hz_recv, hc_send, hc_recv,
+    own_sem, ax_send, ax_recv, fx_send, fx_recv, hz_send, hz_recv, hc_send, hc_recv,
     wz_send, wz_recv, wp_send, wp_recv, wc_send, wc_recv, wq_send, wq_recv,
     kp_send, kp_recv, kz_send, kz_recv, op_send, op_recv,
 ):
@@ -47,7 +47,8 @@
         return lax.rem(cy + t // 2, 2) * 2 + lax.rem(cx + t % 2, 2)
 
     chips = [chip_at(t) for t in range(4)]
-    peers = [(t, k) for t in range(4) for k in range(2) if (t, k) != (0, 0)]
+    every_peer = [(t, k) for t in range(4) for k in range(2) if (t, k) != (0, 0)]
+    peers = [(t, k) for t, k in every_peer if t < 3]
 
     def peer(t, k):
         return chips[t] * 2 + lax.rem(core + k, 2)
@@ -56,11 +57,11 @@
         return lax.rem(row + s, n_row)
 
     barrier = pltpu.get_barrier_semaphore()
-    for t, k in peers:
+    for t, k in every_peer:
         pl.semaphore_signal(barrier, inc=1, device_id=(row, peer(t, k)), device_id_type=MESH)
     for s in range(1, n_row):
         pl.semaphore_signal(barrier, inc=1, device_id=(row_at(s), col), device_id_type=MESH)
-    pl.semaphore_wait(barrier, len(peers) + n_row - 1)
+    pl.semaphore_wait(barrier, len(every_peer) + n_row - 1)
 
     def lanes(c, size):
         return pl.ds(pl.multiple_of(c * size, size), size)
@@ -100,10 +101,30 @@
             halo.at[n, side, own], dst.at[:, pl.ds(at, 1), :, lanes(col, ch)], hc_send.at[n, side, 0, 0]
         )
 
-    def weights_z(s, source):
-        return remote(
-            w_ref, wf.at[:, lanes(core, ch), lanes(source, pair)], wz_send.at[s], wz_recv.at[s], row_at(s), col
-        )
+    half_z = row // 2
+    inner = (row == 1) | (row == 2)
+    beside = row + 1 - 2 * lax.rem(row, 2)
+    across = 2 - half_z
+    far = 3 * (1 - half_z)
+    blocks = [far, across, beside, row]
+
+    def weights_z(source, index, to):
+        part = wf.at[:, lanes(core, ch), lanes(source, pair)]
+        return remote(part, part, wz_send.at[index], wz_recv.at[source], to, col)
+
+    def weights_own(index, to):
+        part = wf.at[:, lanes(core, ch), lanes(row, pair)]
+        return remote(w_ref, part, wz_send.at[index], wz_recv.at[row], to, col)
+
+    def pass_on(n, side):
+        _, dst = arrays[n]
+        part = dst.at[pl.ds(side * (half // 2), half // 2), :, :, lanes(chips[1 + side], pair)]
+        return remote(part, part, fx_send.at[n, side], fx_recv.at[n, side], row, peer(2 - side, 0))
+
+    def passed(n, side):
+        _, dst = arrays[n]
+        part = dst.at[pl.ds(side * (half // 2), half // 2), :, :, lanes(chips[3], pair)]
+        return remote(part, part, fx_send.at[n, side], fx_recv.at[n, side], row, peer(2 - side, 0))
 
     def has(side):
         return has_up if side == 0 else has_down
@@ -128,18 +149,24 @@
     body_copy(1, 0, 1, col).start()
     for t, k in peers:
         body_copy(0, t, k, col).start()
-    for s in range(1, n_row):
-        weights_z(s, row).start()
+    weights_own(0, beside).start()
+
+    @pl.when(inner)
+    def _():
+        weights_own(1, across).start()
+
+    def clear(at):
+        for t in range(3):
+            for grid_ref in (xg, gg):
+                grid_ref[:, at, :, lanes(chips[t], pair)] = jnp.zeros((half, width, pair), BF16)
 
     @pl.when(jnp.logical_not(has_up))
     def _():
-        xg[:, 0] = jnp.zeros((half, width, xg.shape[3]), BF16)
-        gg[:, 0] = jnp.zeros((half, width, xg.shape[3]), BF16)
+        clear(0)
 
     @pl.when(jnp.logical_not(has_down))
     def _():
-        xg[:, height + 1] = jnp.zeros((half, width, xg.shape[3]), BF16)
-        gg[:, height + 1] = jnp.zeros((half, width, xg.shape[3]), BF16)
+        clear(height + 1)
 
     def spread_halo(n):
         for side in range(2):
@@ -151,10 +178,6 @@
                     halo_c(n, side, t, k, col).start()
 
     spread_halo(0)
-    for t, k in peers:
-        if t:
-            body_copy(1, t, k, col).start()
-    spread_halo(1)
 
     own_copies[0].wait()
     own_copies[1].wait()
@@ -187,54 +210,60 @@
         theirs = pl.ds(pl.multiple_of((1 - core) * ch, ch), ch)
         return remote(kgp.at[t, :, theirs], kgr.at[t], kp_send.at[t], kp_recv.at[t], row, mate)
 
+    mine = pl.ds(pl.multiple_of(core * ch, ch), ch)
+
     def z_part(t, to, slot):
-        mine = pl.ds(pl.multiple_of(core * ch, ch), ch)
         return remote(kgp.at[t, :, mine], kgz.at[slot], kz_send.at[t], kz_recv.at[slot], to, col)
 
-    def hand_on(t):
+    def add_in(t, other):
+        def add(i, _):
+            kgp[t, i, mine] = kgp[t, i, mine] + other[i]
+            return 0
+
+        lax.fori_loop(0, taps, add, 0)
+
+    def pair_sum(t):
         mate_part(t).wait_recv()
-        mine = pl.ds(pl.multiple_of(core * ch, ch), ch)
-
-        def add(i, _):
-            kgp[t, i, mine] = kgp[t, i, mine] + kgr[t, i]
-            return 0
-
-        lax.fori_loop(0, taps, add, 0)
-
-        @pl.when(chips[t] != row)
-        def _():
-            z_part(t, chips[t], row).start()
-
-        @pl.when(chips[t] == row)
-        def _():
-            def keep(i, _):
-                kg_ref[i] = kgp[t, i, mine]
-                return 0
-
-            lax.fori_loop(0, taps, keep, 0)
-
-    for t in range(4):
-        for k in range(2):
-            if (t, k) != (0, 0):
-                body_copy(0, t, k, peer(t, k)).wait_recv()
-        wait_halos(0, t)
-
-        def tap_row(a, _):
-            window = xg[:, pl.ds(a, height), :, lanes(chips[t], pair)].reshape(half * height * width, pair)
-            part = jnp.dot(turned[...], window, preferred_element_type=F32)
-            for c in range(3):
-                kgp[t, a * 3 + c] = part[c * pair:(c + 1) * pair]
-            return 0
-
-        lax.fori_loop(0, 3, tap_row, 0)
-        mate_part(t).start()
+        add_in(t, kgr.at[t])
+
+    def relay(t):
+        z_part(t, beside, t).wait_recv()
+        add_in(t, kgz.at[t])
+        z_part(t, blocks[t], 3).start()
+
+    own_copies[2].wait()
+
+    @pl.when(inner)
+    def _():
+        weights_z(beside, 2, across).wait_recv()
+        weights_z(beside, 2, across).start()
+        weights_z(across, 3, beside).wait_recv()
+        weights_z(across, 3, beside).start()
+
+    def neighbours(n):
+        for t in range(3):
+            for k in range(2):
+                if t:
+                    body_copy(n, t, k, peer(t, k)).wait_recv()
+            wait_halos(n, t)
+            if t:
+                pass_on(n, t - 1).start()
+
+    neighbours(0)
+    for t, k in peers:
         if t:
-            hand_on(t - 1)
-    hand_on(3)
-
-    own_copies[2].wait()
-    for s in range(1, n_row):
-        weights_z(s, lax.rem(row + n_row - s, n_row)).wait_recv()
+            body_copy(1, t, k, col).start()
+    spread_halo(1)
+
+    @pl.when(inner)
+    def _():
+        weights_z(far, 4, beside).wait_recv()
+        weights_z(far, 4, beside).start()
+
+    @pl.when(jnp.logical_not(inner))
+    def _():
+        for source in (beside, across, far):
+            weights_z(source, 0, beside).wait_recv()
 
     def weights_mate(k):
         mine = lanes(core if k == 0 else 1 - core, ch)
@@ -251,6 +280,38 @@
     wb_own.start()
     for t in range(1, 4):
         weights_c(t, col).start()
+    body_copy(0, 0, 1, mate).wait_recv()
+    passed(0, 0).wait_recv()
+    passed(0, 1).wait_recv()
+
+    for t in range(4):
+        def tap_row(a, _):
+            window = xg[:, pl.ds(a, height), :, lanes(blocks[t], pair)].reshape(half * height * width, pair)
+            part = jnp.dot(turned[...], window, preferred_element_type=F32)
+            for c in range(3):
+                kgp[t, a * 3 + c] = part[c * pair:(c + 1) * pair]
+            return 0
+
+        lax.fori_loop(0, 3, tap_row, 0)
+        mate_part(t).start()
+        if t:
+            pair_sum(t - 1)
+        if t == 1:
+            @pl.when(jnp.logical_not(inner))
+            def _():
+                z_part(0, beside, 0).start()
+        if t == 3:
+            @pl.when(inner)
+            def _():
+                z_part(2, beside, 2).start()
+    pair_sum(3)
+
+    def keep(i, _):
+        kg_ref[i] = kgp[3, i, mine]
+        return 0
+
+    lax.fori_loop(0, taps, keep, 0)
+    neighbours(1)
 
     def weights_pass(t, k):
         rows = lanes(peer(t, k), ch)
@@ -293,26 +354,40 @@
     convolve(xg, wf, ((1,), (1,)), False, out_ref, 0)
     result_mate(0, out_ref, core).start()
 
+    @pl.when(inner)
+    def _():
+        relay(0)
+
+    @pl.when(jnp.logical_not(inner))
+    def _():
+        z_part(1, beside, 1).start()
+
     wb_own.wait()
     weights_pass(0, 0).start()
     for t in range(1, 4):
         weights_c(t, peer(t, 0)).wait_recv()
         weights_pass(t, 0).start()
-    for t in range(1, 4):
-        for k in range(2):
-            body_copy(1, t, k, peer(t, k)).wait_recv()
-    for t in range(4):
-        wait_halos(1, t)
+    passed(1, 0).wait_recv()
+    passed(1, 1).wait_recv()
     for t in range(4):
         weights_pass(t, 1).wait_recv()
+
+    @pl.when(inner)
+    def _():
+        relay(1)
+
+    @pl.when(jnp.logical_not(inner))
+    def _():
+        z_part(2, beside, 2).start()
+
     convolve(gg, wb, ((1,), (0,)), True, ig_ref, 1)
     result_mate(1, ig_ref, core).start()
 
-    for s in range(1, n_row):
-        z_part(0, row, row_at(s)).wait_recv()
+    for slot in (2, 3):
+        z_part(0, beside, slot).wait_recv()
 
         def add(i, _):
-            kg_ref[i] = kg_ref[i] + kgz[row_at(s), i]
+            kg_ref[i] = kg_ref[i] + kgz[slot, i]
             return 0
 
         lax.fori_loop(0, taps, add, 0)
@@ -329,18 +404,23 @@
             def _():
                 for t, k in peers:
                     halo_c(n, side, t, k, col).wait_send()
-    for s in range(1, n_row):
-        weights_z(s, row).wait_send()
+        for side in range(2):
+            pass_on(n, side).wait_send()
+    weights_own(0, beside).wait_send()
+
+    @pl.when(inner)
+    def _():
+        for index in range(1, 5):
+            weights_own(index, beside).wait_send()
+
     weights_mate(0).wait_send()
     for t in range(1, 4):
         weights_c(t, col).wait_send()
     for t in range(4):
         weights_pass(t, 0).wait_send()
         mate_part(t).wait_send()
-
-        @pl.when(chips[t] != row)
-        def _():
-            z_part(t, chips[t], row).wait_send()
+        if t < 3:
+            z_part(t, beside, t).wait_send()
 
     result_mate(0, out_ref, core).wait_send()
     result_mate(1, ig_ref, core).wait_send()
@@ -380,8 +460,9 @@
             dma((4,)),
             dma((2, 4, 2)), dma((2, 4, 2)),
             dma((2, 2)), dma((2, 2)),
+            dma((2, 2)), dma((2, 2)),
             dma((2, 2, 4, 2)), dma((2, 2, 4, 2)),
-            dma((n_row,)), dma((n_row,)),
+            dma((5,)), dma((n_row,)),
             dma, dma,
             dma((4,)), dma((4,)),
             dma((4,)), dma((4,)),
@@ -399,7 +480,7 @@
 def fits(n_row, n_col, images, kernel_block):
     ch = images.shape[2] // W
     return (
-        n_row == 4 and n_col == 8 and ch == 128 and images.shape[0] % 2 == 0
+        n_row == 4 and n_col == 8 and ch == 128 and images.shape[0] % 4 == 0
         and kernel_block.shape[2] == ch and kernel_block.shape[3] == 2 * ch and images.size <= 8 * 8 * 8192
     )
 

time: 196 us -> 168 us (0.86); the launches traced: 194 us -> 168 us
  Pallas kernels: 175 us -> 149 us
    pallas_call x1, Pallas kernels: 175 us -> 149 us  [fused(): pl.pallas_call(functools.partial(kernel, n_row), out_shape=(jax.ShapeDtyp...]
where the time goes in v1:
time: 168 us
  Pallas kernels  149 us (89%)
  local copies, waits for them, and re-layouts  17.9 us (11%)
    pallas_call x1, Pallas kernels, fused(): pl.pallas_call(functools.partial(kernel, n_row), out_shape=(jax.ShapeDtyp...  149 us
    reshape x4, local copies, waits for them, and re-layouts, to_maps(): return flat.reshape(flat.shape[0], flat.shape[1], flat.shape[2] // W, W)  8.76 us
    reshape x2, local copies, waits for them, and re-layouts, to_flat(): maps.reshape(maps.shape[0], maps.shape[1], maps.shape[2] * maps.shape[3])  4.97 us

profile of v1, /device:TPU:8, one launch (start us, length us, event | category | flops | bytes accessed | tf_op | source)
XLA Modules:
  0.0 167.9 jit_solution(4321015388276399501)
XLA Ops:
  0.6 3.3 %reshape.24 = bf16[8,8,128,64]{3,2,1,0:T(8,128)(2,1)S(1)} reshape(bf16[8,8,8192]{2,1,0:T(8,128)(2,1)} %param.3) | data formatting | bytes 2097152 | tf_op jit(solution)/shard_map/reshape | solution.py:521
  3.9 0.0 copy-start.1
  3.9 1.6 copy.6
  5.5 0.0 copy-done.1
  5.5 2.3 %reshape.25 = bf16[8,8,128,64]{3,2,1,0:T(8,128)(2,1)S(1)} reshape(bf16[8,8,8192]{2,1,0:T(8,128)(2,1)S(1)} %copy-done.1) | data formatting | bytes 2097152 | tf_op jit(solution)/shard_map/reshape | solution.py:521
  7.8 1.6 copy.7
  9.4 149.4 %shard_map.58 = (bf16[8,8,64,128]{3,2,1,0:T(8,128)(2,1)}, bf16[8,8,64,128]{3,2,1,0:T(8,128)(2,1)}, f32[9,128,256]{2,1,0:T(8,128)}) custom-call(bf16[8,8,64,128]{3,2,1,0:T(8,128)(2,1)} %bitcast.12, bf16[8,8,64,128]{3,2,1,0:T(8,128)(2,1)} %bitcast.13, bf16[9,128,256]{2,1,0:T(8,128)(2,1)} %bitcast.15), custom_call_target="tpu_custom_call" | custom-call | flops 28991029248 | bytes 8388608 | tf_op jit(solution)/shard_map/pallas_call | solution.py:440
  158.8 2.0 %copy.9 = bf16[8,8,128,64]{3,2,1,0:T(8,128)(2,1)S(1)} copy(bf16[8,8,128,64]{2,3,1,0:T(8,128)(2,1)} %bitcast.14) | data formatting | bytes 2097152 | tf_op jit(solution)/shard_map/transpose | solution.py:493
  160.8 0.0 copy-start.2
  160.9 2.5 %reshape.28 = bf16[8,8,8192]{2,1,0:T(8,128)(2,1)} reshape(bf16[8,8,128,64]{3,2,1,0:T(8,128)(2,1)S(1)} %copy.9) | data formatting | bytes 2097152 | tf_op jit(solution)/shard_map/reshape | solution.py:525
  163.3 0.0 copy-done.2
  163.3 1.1 copy.8
  164.4 0.0 copy-start
  164.4 2.5 %reshape.27 = bf16[8,8,8192]{2,1,0:T(8,128)(2,1)} reshape(bf16[8,8,128,64]{3,2,1,0:T(8,128)(2,1)S(1)} %copy.8) | data formatting | bytes 2097152 | tf_op jit(solution)/shard_map/reshape | solution.py:525
  166.9 0.0 copy-done
  166.9 1.0 copy.11
Async XLA Ops:
  3.9 1.6 copy-start.1
  160.8 2.5 %copy-start.2 = (bf16[8,8,64,128]{3,2,1,0:T(8,128)(2,1)S(1)}, bf16[8,8,64,128]{3,2,1,0:T(8,128)(2,1)}, u32[]{:S(2)}) copy-start(bf16[8,8,64,128]{3,2,1,0:T(8,128)(2,1)} %get-tuple-element.6) | copy-start | bytes 3145732
  164.4 2.5 %copy-start = (f32[9,128,256]{2,1,0:T(8,128)S(1)}, f32[9,128,256]{2,1,0:T(8,128)}, u32[]{:S(2)}) copy-start(f32[9,128,256]{2,1,0:T(8,128)} %get-tuple-element.8) | copy-start | bytes 3538948

commit v2 on v1

--- a/solution.py
+++ b/solution.py
@@ -29,7 +29,7 @@
 
 def kernel(
     n_row, x_ref, g_ref, w_ref, out_ref, ig_ref, kg_ref,
-    xg, gg, wf, wb, halo, turned, kgp, kgr, kgz, stage,
+    xg, gg, wf, wb, halo, turned, kgp, kgr, kgz, stage, held,
     own_sem, ax_send, ax_recv, fx_send, fx_recv, hz_send, hz_recv, hc_send, hc_recv,
     wz_send, wz_recv, wp_send, wp_recv, wc_send, wc_recv, wq_send, wq_recv,
     kp_send, kp_recv, kz_send, kz_recv, op_send, op_recv,
@@ -317,19 +317,34 @@
         rows = lanes(peer(t, k), ch)
         return remote(wb.at[:, rows], wb.at[:, rows], wq_send.at[t], wq_recv.at[t], row, mate)
 
-    def convolve(grid_ref, weights, dims, flip, result, n):
+    def result_mate(n, result, batch_half, b):
+        return remote(
+            stage.at[n, b], result.at[batch_half * half + b], op_send.at[n, b], op_recv.at[n, b], row, mate
+        )
+
+    def convolve(grid_ref, weights, dims, flip, result, n, parts, start, finish):
         def image(b, _):
             sums = []
             for c in range(3):
                 total = None
                 for a in range(3):
-                    block = grid_ref[b, pl.ds(2 - a if flip else a, height)].reshape(height * width, grid_ref.shape[3])
-                    part = lax.dot_general(block, weights[a * 3 + c], (dims, ((), ())), preferred_element_type=F32)
-                    total = part if total is None else total + part
+                    for t in parts:
+                        at = slice(None) if t is None else lanes(chips[t], pair)
+                        block = grid_ref[b, pl.ds(2 - a if flip else a, height), :, at]
+                        block = block.reshape(height * width, block.shape[2])
+                        tap = weights[a * 3 + c] if t is None else weights[a * 3 + c, at]
+                        part = lax.dot_general(block, tap, (dims, ((), ())), preferred_element_type=F32)
+                        total = part if total is None else total + part
                 sums.append(total)
             if flip:
                 sums = sums[::-1]
-            value = shift_sum(*sums, width).astype(BF16).reshape(height, width, pair)
+            value = shift_sum(*sums, width)
+            if not start:
+                value = value + held[b]
+            if not finish:
+                held[b] = value
+                return 0
+            value = value.astype(BF16).reshape(height, width, pair)
 
             @pl.when(core == 0)
             def _():
@@ -341,18 +356,13 @@
                 result[half + b] = value[:, :, ch:]
                 stage[n, b] = value[:, :, :ch]
 
+            result_mate(n, result, core, b).start()
             return 0
 
         lax.fori_loop(0, half, image, 0)
 
-    def result_mate(n, result, batch_half):
-        return remote(
-            stage.at[n], result.at[pl.ds(batch_half * half, half)], op_send.at[n], op_recv.at[n], row, mate
-        )
-
     weights_mate(1).wait_recv()
-    convolve(xg, wf, ((1,), (1,)), False, out_ref, 0)
-    result_mate(0, out_ref, core).start()
+    convolve(xg, wf, ((1,), (1,)), False, out_ref, 0, (None,), True, True)
 
     @pl.when(inner)
     def _():
@@ -364,24 +374,28 @@
 
     wb_own.wait()
     weights_pass(0, 0).start()
-    for t in range(1, 4):
+    for t in range(1, 3):
         weights_c(t, peer(t, 0)).wait_recv()
         weights_pass(t, 0).start()
+    for t in range(3):
+        weights_pass(t, 1).wait_recv()
+    convolve(gg, wb, ((1,), (0,)), True, ig_ref, 1, (0, 1, 2), True, False)
+    weights_c(3, peer(3, 0)).wait_recv()
+    weights_pass(3, 0).start()
+
+    @pl.when(inner)
+    def _():
+        relay(1)
+
+    @pl.when(jnp.logical_not(inner))
+    def _():
+        z_part(1, beside, 1).wait_send()
+        z_part(2, beside, 2).start()
+
     passed(1, 0).wait_recv()
     passed(1, 1).wait_recv()
-    for t in range(4):
-        weights_pass(t, 1).wait_recv()
-
-    @pl.when(inner)
-    def _():
-        relay(1)
-
-    @pl.when(jnp.logical_not(inner))
-    def _():
-        z_part(2, beside, 2).start()
-
-    convolve(gg, wb, ((1,), (0,)), True, ig_ref, 1)
-    result_mate(1, ig_ref, core).start()
+    weights_pass(3, 1).wait_recv()
+    convolve(gg, wb, ((1,), (0,)), True, ig_ref, 1, (3,), False, True)
 
     for slot in (2, 3):
         z_part(0, beside, slot).wait_recv()
@@ -419,13 +433,20 @@
     for t in range(4):
         weights_pass(t, 0).wait_send()
         mate_part(t).wait_send()
-        if t < 3:
+        if t in (0, 2):
             z_part(t, beside, t).wait_send()
 
-    result_mate(0, out_ref, core).wait_send()
-    result_mate(1, ig_ref, core).wait_send()
-    result_mate(0, out_ref, 1 - core).wait_recv()
-    result_mate(1, ig_ref, 1 - core).wait_recv()
+    @pl.when(inner)
+    def _():
+        z_part(1, beside, 1).wait_send()
+
+    def settle(b, _):
+        for n, result in enumerate((out_ref, ig_ref)):
+            result_mate(n, result, core, b).wait_send()
+            result_mate(n, result, 1 - core, b).wait_recv()
+        return 0
+
+    lax.fori_loop(0, half, settle, 0)
 
 
 def fused(images, upstream, weights):
@@ -457,6 +478,7 @@
             pltpu.VMEM((4, taps, ch, pair), F32),
             pltpu.VMEM((n_row, taps, ch, pair), F32),
             pltpu.VMEM((2, half, height, width, ch), BF16),
+            pltpu.VMEM((half, height * width, pair), F32),
             dma((4,)),
             dma((2, 4, 2)), dma((2, 4, 2)),
             dma((2, 2)), dma((2, 2)),
@@ -468,7 +490,7 @@
             dma((4,)), dma((4,)),
             dma((4,)), dma((4,)),
             dma((4,)), dma((n_row,)),
-            dma((2,)), dma((2,)),
+            dma((2, half)), dma((2, half)),
         ],
         compiler_params=pltpu.CompilerParams(
             collective_id=0, has_side_effects=True, vmem_limit_bytes=60 * 1024 * 1024

time: 168 us -> 165 us (0.982)
  Pallas kernels: 149 us -> 146 us
    pallas_call x1, Pallas kernels: 149 us -> 146 us  [fused(): pl.pallas_call(functools.partial(kernel, n_row), out_shape=(jax.ShapeDtyp...]
where the time goes in v2:
time: 165 us
  Pallas kernels  146 us (88%)
  local copies, waits for them, and re-layouts  17.9 us (11%)
    pallas_call x1, Pallas kernels, fused(): pl.pallas_call(functools.partial(kernel, n_row), out_shape=(jax.ShapeDtyp...  146 us
    reshape x4, local copies, waits for them, and re-layouts, to_maps(): return flat.reshape(flat.shape[0], flat.shape[1], flat.shape[2] // W, W)  8.76 us
    reshape x2, local copies, waits for them, and re-layouts, to_flat(): maps.reshape(maps.shape[0], maps.shape[1], maps.shape[2] * maps.shape[3])  4.97 us

profile of v2, /device:TPU:8, one launch (start us, length us, event | category | flops | bytes accessed | tf_op | source)
XLA Modules:
  0.0 164.8 jit_solution(7817386919619384021)
XLA Ops:
  0.6 3.3 %reshape.24 = bf16[8,8,128,64]{3,2,1,0:T(8,128)(2,1)S(1)} reshape(bf16[8,8,8192]{2,1,0:T(8,128)(2,1)} %param.3) | data formatting | bytes 2097152 | tf_op jit(solution)/shard_map/reshape | solution.py:543
  3.9 0.0 copy-start.1
  3.9 1.6 copy.6
  5.5 0.0 copy-done.1
  5.5 2.3 %reshape.25 = bf16[8,8,128,64]{3,2,1,0:T(8,128)(2,1)S(1)} reshape(bf16[8,8,8192]{2,1,0:T(8,128)(2,1)S(1)} %copy-done.1) | data formatting | bytes 2097152 | tf_op jit(solution)/shard_map/reshape | solution.py:543
  7.8 1.6 copy.7
  9.4 146.3 %shard_map.58 = (bf16[8,8,64,128]{3,2,1,0:T(8,128)(2,1)}, bf16[8,8,64,128]{3,2,1,0:T(8,128)(2,1)}, f32[9,128,256]{2,1,0:T(8,128)}) custom-call(bf16[8,8,64,128]{3,2,1,0:T(8,128)(2,1)} %bitcast.12, bf16[8,8,64,128]{3,2,1,0:T(8,128)(2,1)} %bitcast.13, bf16[9,128,256]{2,1,0:T(8,128)(2,1)} %bitcast.15), custom_call_target="tpu_custom_call" | custom-call | flops 28991029248 | bytes 8388608 | tf_op jit(solution)/shard_map/pallas_call | solution.py:461
  155.7 2.0 %copy.9 = bf16[8,8,128,64]{3,2,1,0:T(8,128)(2,1)S(1)} copy(bf16[8,8,128,64]{2,3,1,0:T(8,128)(2,1)} %bitcast.14) | data formatting | bytes 2097152 | tf_op jit(solution)/shard_map/transpose | solution.py:515
  157.8 0.0 copy-start.2
  157.8 2.5 %reshape.28 = bf16[8,8,8192]{2,1,0:T(8,128)(2,1)} reshape(bf16[8,8,128,64]{3,2,1,0:T(8,128)(2,1)S(1)} %copy.9) | data formatting | bytes 2097152 | tf_op jit(solution)/shard_map/reshape | solution.py:547
  160.3 0.0 copy-done.2
  160.3 1.1 copy.8
  161.3 0.0 copy-start
  161.3 2.5 %reshape.27 = bf16[8,8,8192]{2,1,0:T(8,128)(2,1)} reshape(bf16[8,8,128,64]{3,2,1,0:T(8,128)(2,1)S(1)} %copy.8) | data formatting | bytes 2097152 | tf_op jit(solution)/shard_map/reshape | solution.py:547
  163.8 0.0 copy-done
  163.8 1.0 copy.11
Async XLA Ops:
  3.9 1.6 copy-start.1
  157.8 2.5 %copy-start.2 = (bf16[8,8,64,128]{3,2,1,0:T(8,128)(2,1)S(1)}, bf16[8,8,64,128]{3,2,1,0:T(8,128)(2,1)}, u32[]{:S(2)}) copy-start(bf16[8,8,64,128]{3,2,1,0:T(8,128)(2,1)} %get-tuple-element.6) | copy-start | bytes 3145732
  161.3 2.5 %copy-start = (f32[9,128,256]{2,1,0:T(8,128)S(1)}, f32[9,128,256]{2,1,0:T(8,128)}, u32[]{:S(2)}) copy-start(f32[9,128,256]{2,1,0:T(8,128)} %get-tuple-element.8) | copy-start | bytes 3538948

commit v3 on v2

--- a/solution.py
+++ b/solution.py
@@ -311,6 +311,15 @@
         return 0
 
     lax.fori_loop(0, taps, keep, 0)
+    @pl.when(inner)
+    def _():
+        relay(0)
+
+    @pl.when(jnp.logical_not(inner))
+    def _():
+        z_part(0, beside, 0).wait_send()
+        z_part(1, beside, 1).start()
+
     neighbours(1)
 
     def weights_pass(t, k):
@@ -364,33 +373,25 @@
     weights_mate(1).wait_recv()
     convolve(xg, wf, ((1,), (1,)), False, out_ref, 0, (None,), True, True)
 
-    @pl.when(inner)
-    def _():
-        relay(0)
-
-    @pl.when(jnp.logical_not(inner))
-    def _():
-        z_part(1, beside, 1).start()
-
     wb_own.wait()
     weights_pass(0, 0).start()
     for t in range(1, 3):
         weights_c(t, peer(t, 0)).wait_recv()
         weights_pass(t, 0).start()
+    @pl.when(inner)
+    def _():
+        relay(1)
+
+    @pl.when(jnp.logical_not(inner))
+    def _():
+        z_part(1, beside, 1).wait_send()
+        z_part(2, beside, 2).start()
+
     for t in range(3):
         weights_pass(t, 1).wait_recv()
     convolve(gg, wb, ((1,), (0,)), True, ig_ref, 1, (0, 1, 2), True, False)
     weights_c(3, peer(3, 0)).wait_recv()
     weights_pass(3, 0).start()
-
-    @pl.when(inner)
-    def _():
-        relay(1)
-
-    @pl.when(jnp.logical_not(inner))
-    def _():
-        z_part(1, beside, 1).wait_send()
-        z_part(2, beside, 2).start()
 
     passed(1, 0).wait_recv()
     passed(1, 1).wait_recv()
@@ -433,12 +434,13 @@
     for t in range(4):
         weights_pass(t, 0).wait_send()
         mate_part(t).wait_send()
-        if t in (0, 2):
+
+    z_part(2, beside, 2).wait_send()
+
+    @pl.when(inner)
+    def _():
+        for t in range(2):
             z_part(t, beside, t).wait_send()
-
-    @pl.when(inner)
-    def _():
-        z_part(1, beside, 1).wait_send()
 
     def settle(b, _):
         for n, result in enumerate((out_ref, ig_ref)):

time: 165 us -> 161 us (0.976)
  Pallas kernels: 146 us -> 141 us
    pallas_call x1, Pallas kernels: 146 us -> 141 us  [fused(): pl.pallas_call(functools.partial(kernel, n_row), out_shape=(jax.ShapeDtyp...]
where the time goes in v3:
time: 161 us; the launch traced here: 160 us
  Pallas kernels  141 us (88%)
  local copies, waits for them, and re-layouts  17.9 us (11%)
    pallas_call x1, Pallas kernels, fused(): pl.pallas_call(functools.partial(kernel, n_row), out_shape=(jax.ShapeDtyp...  141 us
    reshape x4, local copies, waits for them, and re-layouts, to_maps(): return flat.reshape(flat.shape[0], flat.shape[1], flat.shape[2] // W, W)  8.76 us
    reshape x2, local copies, waits for them, and re-layouts, to_flat(): maps.reshape(maps.shape[0], maps.shape[1], maps.shape[2] * maps.shape[3])  4.97 us

profile of v3, /device:TPU:8, one launch (start us, length us, event | category | flops | bytes accessed | tf_op | source)
XLA Modules:
  0.0 160.0 jit_solution(15751170044531295207)
XLA Ops:
  0.6 3.3 %reshape.24 = bf16[8,8,128,64]{3,2,1,0:T(8,128)(2,1)S(1)} reshape(bf16[8,8,8192]{2,1,0:T(8,128)(2,1)} %param.3) | data formatting | bytes 2097152 | tf_op jit(solution)/shard_map/reshape | solution.py:545
  3.9 0.0 copy-start.1
  3.9 1.6 %copy.6 = bf16[8,8,128,64]{2,3,1,0:T(8,128)(2,1)} copy(bf16[8,8,128,64]{3,2,1,0:T(8,128)(2,1)S(1)} %reshape.24) | data formatting | bytes 2097152 | tf_op jit(solution)/shard_map/reshape | solution.py:545
  5.5 0.0 copy-done.1
  5.5 2.3 %reshape.25 = bf16[8,8,128,64]{3,2,1,0:T(8,128)(2,1)S(1)} reshape(bf16[8,8,8192]{2,1,0:T(8,128)(2,1)S(1)} %copy-done.1) | data formatting | bytes 2097152 | tf_op jit(solution)/shard_map/reshape | solution.py:545
  7.8 1.6 %copy.7 = bf16[8,8,128,64]{2,3,1,0:T(8,128)(2,1)} copy(bf16[8,8,128,64]{3,2,1,0:T(8,128)(2,1)S(1)} %reshape.25) | data formatting | bytes 2097152 | tf_op jit(solution)/shard_map/reshape | solution.py:545
  9.4 141.5 %shard_map.58 = (bf16[8,8,64,128]{3,2,1,0:T(8,128)(2,1)}, bf16[8,8,64,128]{3,2,1,0:T(8,128)(2,1)}, f32[9,128,256]{2,1,0:T(8,128)}) custom-call(bf16[8,8,64,128]{3,2,1,0:T(8,128)(2,1)} %bitcast.12, bf16[8,8,64,128]{3,2,1,0:T(8,128)(2,1)} %bitcast.13, bf16[9,128,256]{2,1,0:T(8,128)(2,1)} %bitcast.15), custom_call_target="tpu_custom_call" | custom-call | flops 28991029248 | bytes 8388608 | tf_op jit(solution)/shard_map/pallas_call | solution.py:463
  150.9 2.0 %copy.9 = bf16[8,8,128,64]{3,2,1,0:T(8,128)(2,1)S(1)} copy(bf16[8,8,128,64]{2,3,1,0:T(8,128)(2,1)} %bitcast.14) | data formatting | bytes 2097152 | tf_op jit(solution)/shard_map/transpose | solution.py:517
  152.9 0.0 copy-start.2
  153.0 2.5 %reshape.28 = bf16[8,8,8192]{2,1,0:T(8,128)(2,1)} reshape(bf16[8,8,128,64]{3,2,1,0:T(8,128)(2,1)S(1)} %copy.9) | data formatting | bytes 2097152 | tf_op jit(solution)/shard_map/reshape | solution.py:549
  155.4 0.0 copy-done.2
  155.4 1.1 copy.8
  156.5 0.0 copy-start
  156.5 2.5 %reshape.27 = bf16[8,8,8192]{2,1,0:T(8,128)(2,1)} reshape(bf16[8,8,128,64]{3,2,1,0:T(8,128)(2,1)S(1)} %copy.8) | data formatting | bytes 2097152 | tf_op jit(solution)/shard_map/reshape | solution.py:549
  159.0 0.0 copy-done
  159.0 1.0 copy.11
Async XLA Ops:
  3.9 1.6 %copy-start.1 = (bf16[8,8,8192]{2,1,0:T(8,128)(2,1)S(1)}, bf16[8,8,8192]{2,1,0:T(8,128)(2,1)}, u32[]{:S(2)}) copy-start(bf16[8,8,8192]{2,1,0:T(8,128)(2,1)} %param.5) | copy-start | bytes 3145732
  152.9 2.5 %copy-start.2 = (bf16[8,8,64,128]{3,2,1,0:T(8,128)(2,1)S(1)}, bf16[8,8,64,128]{3,2,1,0:T(8,128)(2,1)}, u32[]{:S(2)}) copy-start(bf16[8,8,64,128]{3,2,1,0:T(8,128)(2,1)} %get-tuple-element.6) | copy-start | bytes 3145732
  156.5 2.5 %copy-start = (f32[9,128,256]{2,1,0:T(8,128)S(1)}, f32[9,128,256]{2,1,0:T(8,128)}, u32[]{:S(2)}) copy-start(f32[9,128,256]{2,1,0:T(8,128)} %get-tuple-element.8) | copy-start | bytes 3538948
